TPU v7x, 256 devices: a whole 4x4x8 slice. The times are simulated.
256 devices in a mesh: sky: 16 (over x, y), freq: 16 (over z, core).
Axes of the slice: x: 4, y: 4, z: 8, core: 2. Of those that a mesh axis runs over, the one named last changes fastest.
Arguments:
- pieces: bfloat16 [128, 128, 128, 128], P('sky', 'freq'), may hold values from -120 to 120
- beam: bfloat16 [128, 128, 128], P('sky'), may hold values from 0.099609375 to 1
- destination: int32 [128], P('sky'), may hold values from 0 to 63, as said below
- clip_tenths: int32 [3, 4], replicated, may hold values from 30 to 60
Outputs:
- significance: float32 [128, 2048, 512], P('freq', 'sky')
Inputs may be any that keep to these rules, and one draw needn't show every extreme that they name: Among the 8 pieces of one index of sky, at most 2 have destinations in one tile, that is with equal destination // 4. In every draw some tile receives exactly 2 pieces from every index of sky.
All inputs are finite; a program needn't handle non-finite values.
Results may differ from a plain program's by a relative error of at most 0.0036.
Values may be sent and summed in bfloat16 or wider, within the bound.
A program may use at most 128 MiB of HBM per device.

v0:
```python
import jax
import jax.numpy as jnp
from jax import lax
from jax.sharding import PartitionSpec as P

ROWB = 1
COLB = 4
RIM = 8
EDGE = 7
KERNELS = 3
REGULARIZER = 0.05
EPSILON = 1e-06
KERNEL_FWHM = (3.0, 6.0, 9.0)
HALF_WIDTHS = (0, 1, 3, 7)


def extended(block, sides, width):
    for axis, dim in sides:
        count = lax.axis_size(axis)
        forward = [(i, i + 1) for i in range(count - 1)]
        backward = [(target, source) for source, target in forward]
        low = lax.ppermute(
            lax.slice_in_dim(block, block.shape[dim] - width, None, axis=dim), axis, forward
        )
        high = lax.ppermute(lax.slice_in_dim(block, 0, width, axis=dim), axis, backward)
        block = jnp.concatenate([low, block, high], axis=dim)
    return block


def kernel_taps(kernel):
    offsets = jnp.arange(-RIM, RIM + 1).astype(jnp.float32)
    sigma = KERNEL_FWHM[kernel] / 2.3548
    return jnp.exp(-offsets * offsets / (2.0 * sigma * sigma)).astype(jnp.bfloat16)


def band_matrix(weights, rows_out, rows_in, shift):
    outer = jnp.arange(rows_out)[:, None]
    inner = jnp.arange(rows_in)[None, :]
    offset = inner - shift - outer
    inside = jnp.abs(offset) <= RIM
    picked = weights[jnp.clip(offset + RIM, 0, 2 * RIM)]
    return jnp.where(inside, picked, jnp.zeros_like(picked))


def smooth(padded, kernel):
    weights = kernel_taps(kernel)
    tall = padded.shape[1] - 2 * RIM
    broad = padded.shape[2]
    across_matrix = band_matrix(weights, broad, broad, 0)
    down_matrix = band_matrix(weights, tall, tall + 2 * RIM, RIM)
    across = jnp.einsum(
        "cyx,zx->cyz", padded, across_matrix, preferred_element_type=jnp.float32
    ).astype(jnp.bfloat16)
    return jnp.einsum(
        "vy,cyz->cvz", down_matrix, across, preferred_element_type=jnp.float32
    ).astype(jnp.bfloat16)


def boxcars(layer):
    channels = layer.shape[0] - 2 * EDGE
    running = layer[EDGE : EDGE + channels].astype(jnp.float32)
    found = [running]
    for step in range(1, EDGE + 1):
        running = (
            running
            + layer[EDGE - step : EDGE - step + channels].astype(jnp.float32)
            + layer[EDGE + step : EDGE + step + channels].astype(jnp.float32)
        )
        if step in HALF_WIDTHS:
            found.append(running)
    return found


def kernel_boxcars(layer):
    found = boxcars(layer)
    power = jnp.stack([jnp.sum(item * item, axis=(1, 2)) for item in found])
    return (found, power)


def raise_score(best, found, totals, thresholds, cells):
    noise_level = jnp.sqrt(totals / cells + EPSILON)
    factor = 10.0 / (thresholds.astype(jnp.float32)[:, None] * noise_level)
    for width, running in enumerate(found):
        best = jnp.maximum(best, jnp.abs(running) * factor[width][:, None, None])
    return best


def owner_tables(beams_in, labels_in, tile_blocks):
    onehot = labels_in[None, :] == jnp.arange(tile_blocks)[:, None]
    beam_wide = beams_in.astype(jnp.float32)
    coverage = (
        jnp.einsum(
            "bs,syx->byx",
            onehot.astype(jnp.float32),
            beam_wide * beam_wide,
            precision=lax.Precision.HIGHEST,
        )
        + REGULARIZER
    )
    return (onehot.astype(jnp.bfloat16), coverage)


def block_values(onehot, coverage, arrived):
    numerator = jnp.einsum("bs,scyx->bcyx", onehot, arrived, preferred_element_type=jnp.float32)
    return (numerator / coverage[:, None]).astype(jnp.bfloat16)


def shards(pieces, beam, destination, clip_tenths):
    sky_count = lax.axis_size("sky")
    piece_count, channels, block_size, _ = pieces.shape
    tile_blocks = ROWB * COLB
    capacity = max(2, 2 * piece_count // sky_count)
    slot_total = sky_count * capacity
    owners = destination // tile_blocks
    numbering = jnp.arange(piece_count)
    earlier = (owners[None, :] == owners[:, None]) & (numbering[None, :] < numbering[:, None])
    position = jnp.sum(earlier.astype(jnp.int32), axis=1)
    slot_index = owners * capacity + position
    weighted = (beam[:, None].astype(jnp.float32) * pieces.astype(jnp.float32)).astype(jnp.bfloat16)
    outgoing = (
        jnp.zeros((slot_total, channels, block_size, block_size), jnp.bfloat16)
        .at[slot_index]
        .set(weighted)
    )
    beams_out = (
        jnp.zeros((slot_total, block_size, block_size), jnp.bfloat16).at[slot_index].set(beam)
    )
    labels_out = (
        jnp.full((slot_total,), -1, jnp.int32).at[slot_index].set(destination % tile_blocks)
    )
    arrived, beams_in, labels_in = (
        lax.all_to_all(outgoing, "sky", split_axis=0, concat_axis=0, tiled=True),
        lax.all_to_all(beams_out, "sky", split_axis=0, concat_axis=0, tiled=True),
        lax.all_to_all(labels_out, "sky", split_axis=0, concat_axis=0, tiled=True),
    )
    onehot, coverage = owner_tables(beams_in, labels_in, tile_blocks)
    tile_values = block_values(onehot, coverage, arrived)
    combined = tile_values.reshape(ROWB, COLB, channels, block_size, block_size).transpose(
        2, 0, 3, 1, 4
    )
    combined = combined.reshape(channels, ROWB * block_size, COLB * block_size)
    padded = extended(combined, (("sky", 1),), RIM)
    smoothed = jnp.stack([smooth(padded, kernel) for kernel in range(KERNELS)])
    planes = extended(smoothed, (("freq", 1),), EDGE)
    cells = float(sky_count * ROWB * block_size * COLB * block_size)
    best = jnp.zeros((channels, ROWB * block_size, COLB * block_size), jnp.float32)
    results = [kernel_boxcars(planes[kernel]) for kernel in range(KERNELS)]
    powers = jnp.stack([item[1] for item in results])
    totals = lax.psum(powers, "sky")
    for kernel in range(KERNELS):
        best = raise_score(best, results[kernel][0], totals[kernel], clip_tenths[kernel], cells)
    return best


def solution(mesh):
    return jax.shard_map(
        shards,
        mesh=mesh,
        in_specs=(P("sky", "freq", None, None), P("sky", None, None), P("sky"), P()),
        out_specs=P("freq", "sky", None),
        check_vma=False,
    )
```

profile of v0, /device:TPU:136, one launch (start us, length us, event | category | flops | bytes accessed | tf_op | source)
XLA Modules:
  0.0 326.6 jit_solution(16188896289594419364)
XLA Ops:
  0.0 0.0 copy-start.5
  0.0 0.7 and_select_fusion
  0.7 0.2 convert_reduce_fusion
  0.9 0.6 scatter_custom_fusion
  1.5 0.7 all_to_all.12
  2.2 7.4 %all-to-all-start = ((s32[16,2,1]{1,2,0:T(1,128)}), s32[16,2,1]{1,2,0:T(1,128)S(1)}, u32[]{:S(2)}, u32[]{:S(2)}) async-start(s32[16,2,1]{1,2,0:T(1,128)} %bitcast), calls=%async_computation | async-start | bytes 16384 | tf_op jit(solution)/shard_map/all_to_all | solution.py:134
  9.6 1.2 broadcast_in_dim.13
  10.8 2.4 scatter_fusion.1
  13.2 2.6 all-to-all-done
  15.8 4.9 %all-to-all-start.2 = ((bf16[32,128,128]{2,1,0:T(8,128)(2,1)}), bf16[32,128,128]{2,1,0:T(8,128)(2,1)S(1)}, u32[]{:S(2)}, u32[]{:S(2)}) async-start(bf16[32,128,128]{2,1,0:T(8,128)(2,1)} %scatter_fusion.1), calls=%async_computation.2 | async-start | bytes 2097152 | tf_op jit(solution)/shard_map/all_to_all | solution.py:133
  20.7 0.0 copy-done.5
  20.7 2.2 multiply_convert_fusion
  22.9 5.3 %broadcast_in_dim.12 = bf16[32,8,128,128]{3,2,1,0:T(8,128)(2,1)} broadcast(bf16[]{:T(256)} %constant.32.clone.1), dimensions={} | broadcast | bytes 8388610 | tf_op jit(solution)/shard_map/broadcast_in_dim | solution.py:121
  28.3 5.0 %scatter_fusion = bf16[32,8,128,128]{3,2,1,0:T(8,128)(2,1)} fusion(bf16[32,8,128,128]{3,2,1,0:T(8,128)(2,1)} %broadcast_in_dim.12, s32[8]{0:T(128)S(1)} %compare_select_fusion.2, bf16[8,8,128,128]{3,2,1,0:T(8,128)(2,1)S(1)} %multiply_convert_fusion), kind=kCustom, calls=%fused_computation.1 | custom fusion | bytes 6291488 | tf_op jit(solution)/shard_map/scatter | solution.py:123
  33.3 2.4 all-to-all-done.2
  35.7 5.9 %all-to-all-start.1 = ((bf16[32,8,128,128]{3,2,1,0:T(8,128)(2,1)}), bf16[32,8,128,128]{3,2,1,0:T(8,128)(2,1)}, u32[]{:S(2)}, u32[]{:S(2)}) async-start(bf16[32,8,128,128]{3,2,1,0:T(8,128)(2,1)} %scatter_fusion), calls=%async_computation.1 | async-start | bytes 16777216 | tf_op jit(solution)/shard_map/all_to_all | solution.py:132
  41.7 0.7 fusion.681
  42.4 0.7 fusion.680
  43.1 0.7 fusion.679
  43.8 0.5 broadcast.2173
  44.3 0.7 reduce.3
  45.0 0.1 eq.33
  45.1 0.2 convert_multiply_fusion.3
  45.4 2.0 fusion.25
  47.3 121.8 %all-to-all-done.1 = bf16[32,8,128,128]{3,2,1,0:T(8,128)(2,1)} async-done(((bf16[32,8,128,128]{3,2,1,0:T(8,128)(2,1)}), bf16[32,8,128,128]{3,2,1,0:T(8,128)(2,1)}, u32[]{:S(2)}, u32[]{:S(2)}) %all-to-all-start.1) | async-done | bytes 8388640 | tf_op jit(solution)/shard_map/all_to_all | solution.py:132
  169.2 8.3 %fusion.54 = bf16[8,1,128,4,128]{4,3,2,0,1:T(4,128)(2,1)S(1)} fusion(f32[4,128,128]{2,0,1:T(4,128)S(1)} %fusion.25, bf16[32,8,128,128]{3,2,1,0:T(8,128)(2,1)} %all-to-all-done.1, s32[32]{0:T(128)S(1)} %eq.33), kind=kOutput, calls=%fused_computation.165 | convolution fusion | flops 34603136 | bytes 9699456 | tf_op jit(solution)/shard_map/bs,scyx->bcyx/dot_general | solution.py:104
  177.5 0.4 reshape.273
  177.9 1.9 collective-permute-start
  179.9 4.1 %collective-permute-start.1 = (bf16[8,8,512]{2,1,0:T(8,128)(2,1)S(1)}, bf16[8,8,512]{2,1,0:T(8,128)(2,1)S(1)}, u32[]{:S(2)}, u32[]{:S(2)}) collective-permute-start(bf16[8,8,512]{2,1,0:T(8,128)(2,1)S(1)} %get-tuple-element.33), channel_id=1, source_target_pairs={{16,0},{32,16},{48,32},{64,48},{80,64},{96,80},{112,96},{128,112},... | collective-permute-start | bytes 196616 | tf_op jit(solution)/shard_map/ppermute | solution.py:25
  184.0 0.1 collective-permute-done
  184.1 0.1 constant_dynamic-update-slice_fusion.1
  184.2 1.8 collective-permute-done.1
  186.0 0.0 copy-start.6
  186.0 12.4 %convolution_convert_fusion.4 = bf16[8,512,128]{2,1,0:T(8,128)(2,1)S(1)} fusion(bf16[8,144,512]{2,1,0:T(8,128)(2,1)S(1)} %constant_dynamic-update-slice_fusion, bf16[]{:T(256)} %bitcast.61, bf16[]{:T(256)} %bitcast.62, bf16[]{:T(256)} %bitcast.63, bf16[]{:T(256)} %bitcast.64, bf16[]{:T(256)} %bitcast.65, bf16[]{:T(256)} %bitcast.67, bf16[]{:T(256)} %bitcast.66, ...), kind=kOutput, calls=%fused_computation.93 | convolution fusion | flops 767873024 | bytes 2228834 | tf_op jit(solution)/shard_map/vy,cyz->cvz/dot_general | solution.py:54
  198.4 0.0 copy-done.6
  198.4 12.2 %convolution_convert_fusion.5 = bf16[8,512,128]{2,1,0:T(8,128)(2,1)S(1)} fusion(bf16[8,144,512]{2,1,0:T(8,128)(2,1)S(1)} %constant_dynamic-update-slice_fusion, bf16[]{:T(256)} %bitcast.26, bf16[]{:T(256)} %bitcast.27, bf16[]{:T(256)} %bitcast.28, bf16[]{:T(256)} %bitcast.29, bf16[]{:T(256)} %bitcast.30, bf16[]{:T(256)} %bitcast.32, bf16[]{:T(256)} %bitcast.31, ...), kind=kOutput, calls=%fused_computation.94 | convolution fusion | flops 767873024 | bytes 2228834 | tf_op jit(solution)/shard_map/vy,cyz->cvz/dot_general | solution.py:54
  210.6 13.5 %convolution_convert_fusion.3 = bf16[8,512,128]{2,1,0:T(8,128)(2,1)S(1)} fusion(bf16[8,144,512]{2,1,0:T(8,128)(2,1)} %copy-done.6, bf16[]{:T(256)} %bitcast.84, bf16[]{:T(256)} %bitcast.85, bf16[]{:T(256)} %bitcast.86, bf16[]{:T(256)} %bitcast.87, bf16[]{:T(256)} %bitcast.88, bf16[]{:T(256)} %bitcast.90, bf16[]{:T(256)} %bitcast.89, bf16[]{:T(256)} %bitcast.74, ...), kind=kOutput, calls=%fused_computation.92 | convolution fusion | flops 767873024 | bytes 2228834 | tf_op jit(solution)/shard_map/vy,cyz->cvz/dot_general | solution.py:54
  224.1 0.3 pad_maximum_fusion.1
  224.5 0.0 copy-start.7
  224.5 1.2 fusion.677
  225.7 1.9 collective-permute-start.2
  227.7 5.1 %collective-permute-start.3 = (bf16[3,7,128,512]{2,3,1,0:T(8,128)(2,1)S(1)}, bf16[3,7,128,512]{2,3,1,0:T(8,128)(2,1)S(1)}, u32[]{:S(2)}, u32[]{:S(2)}) collective-permute-start(bf16[3,7,128,512]{2,3,1,0:T(8,128)(2,1)S(1)} %get-tuple-element.32), channel_id=1, source_target_pairs={{1,0},{2,1},{3,2},{4,3},{5,4},{6,5},{7,6},{8,7},{9,8},{10,9},{11,1... | collective-permute-start | bytes 8257544 | tf_op jit(solution)/shard_map/ppermute | solution.py:25
  232.8 0.0 copy-done.7
  232.8 28.6 %collective-permute-done.2 = bf16[3,7,128,512]{2,3,1,0:T(8,128)(2,1)S(1)} collective-permute-done((bf16[3,7,128,512]{2,3,1,0:T(8,128)(2,1)S(1)}, bf16[3,7,128,512]{2,3,1,0:T(8,128)(2,1)S(1)}, u32[]{:S(2)}, u32[]{:S(2)}) %collective-permute-start.2) | collective-permute-done | bytes 2752544 | tf_op jit(solution)/shard_map/ppermute | solution.py:22
  261.3 1.8 collective-permute-done.3
  263.1 1.2 maximum_maximum_fusion
  264.3 0.0 copy-start
  264.3 0.0 copy-start.1
  264.3 1.2 multiply_reduce_fusion.4
  265.5 0.0 copy-start.3
  265.5 3.1 multiply_reduce_fusion.8
  268.6 0.0 copy-start.2
  268.6 0.0 copy-done.3
  268.6 3.6 %multiply_reduce_fusion.7 = (f32[8]{0:T(128)S(1)}, f32[8,128,512]{1,2,0:T(8,128)S(1)}, f32[8]{0:T(128)S(1)}, f32[8,128,512]{1,2,0:T(8,128)}) fusion(bf16[3,15,128,512]{2,3,1,0:T(8,128)(2,1)S(1)} %get-tuple-element.30, bf16[3,15,128,512]{2,3,1,0:T(8,128)(2,1)S(1)} %get-tuple-element.29, bf16[8,512,128]{2,1,0:T(8,128)(2,1)S(1)} %convolution_convert_fusion.5, ...), kind=kLoop, calls=%fused_computation.85 | loop fusion | flops 17301488 | bytes 22020160 | tf_op jit(solution)/shard_map/reduce_sum | solution.py:76
  272.2 0.0 copy-start.4
  272.2 0.0 copy-done
  272.2 0.0 copy-done.1
  272.2 0.0 copy-done.2
  272.2 4.1 %multiply_reduce_fusion.6 = (f32[8]{0:T(128)S(1)}, f32[8,128,512]{1,2,0:T(8,128)}, f32[8]{0:T(128)S(1)}, f32[8,128,512]{1,2,0:T(8,128)}) fusion(bf16[3,15,128,512]{2,3,1,0:T(8,128)(2,1)S(1)} %get-tuple-element.30, bf16[3,15,128,512]{2,3,1,0:T(8,128)(2,1)S(1)} %get-tuple-element.29, f32[8,128,512]{1,2,0:T(8,128)S(1)} %get-tuple-element.12, ...), kind=kLoop, calls=%fused_computation.84 | loop fusion | flops 18874352 | bytes 25165888 | tf_op jit(solution)/shard_map/reduce_sum | solution.py:76
  276.4 0.0 copy-done.4
  276.4 38.0 %psum.7 = f32[3,4,8]{2,1,0:T(4,128)S(1)} all-reduce(f32[3,4,8]{2,1,0:T(4,128)S(1)} %pad_maximum_fusion.2), channel_id=1, replica_groups=mesh['sky'=16,'freq'=16] {'sky'}, use_global_device_ids=true, to_apply=%region_16.17 | all-reduce | flops 96 | bytes 768 | tf_op jit(solution)/shard_map/psum | solution.py:149
  314.4 0.1 fusion.554
  314.5 9.2 %fusion.14 = f32[8,128,512]{1,2,0:T(8,128)} fusion(f32[8,128,512]{1,2,0:T(8,128)} %get-tuple-element.26, f32[8,128,512]{1,2,0:T(8,128)} %copy-done.2, f32[8,128,512]{1,2,0:T(8,128)} %get-tuple-element.28, f32[8,128,512]{1,2,0:T(8,128)} %copy-done.3, f32[8,128,512]{1,2,0:T(8,128)} %get-tuple-element.14, f32[8,128,512]{1,2,0:T(8,128)} %copy-done.4, ...), kind=kLoop, calls=%fused_computation.31 | loop fusion | flops 26738688 | bytes 24117632 | tf_op jit(solution)/shard_map/max | solution.py:84
  323.7 2.9 copy.18
  (16 shorter events, 0.2 us)
Async XLA Ops:
  0.0 20.7 %copy-start.5 = (bf16[8,128,128]{2,1,0:T(8,128)(2,1)S(1)}, bf16[8,128,128]{2,1,0:T(8,128)(2,1)}, u32[]{:S(2)}) copy-start(bf16[8,128,128]{2,1,0:T(8,128)(2,1)} %param.5) | copy-start | bytes 786436
  2.2 13.6 %all-to-all-start = ((s32[16,2,1]{1,2,0:T(1,128)}), s32[16,2,1]{1,2,0:T(1,128)S(1)}, u32[]{:S(2)}, u32[]{:S(2)}) async-start(s32[16,2,1]{1,2,0:T(1,128)} %bitcast), calls=%async_computation | async-start | bytes 16384 | tf_op jit(solution)/shard_map/all_to_all | solution.py:134
  15.8 19.9 %all-to-all-start.2 = ((bf16[32,128,128]{2,1,0:T(8,128)(2,1)}), bf16[32,128,128]{2,1,0:T(8,128)(2,1)S(1)}, u32[]{:S(2)}, u32[]{:S(2)}) async-start(bf16[32,128,128]{2,1,0:T(8,128)(2,1)} %scatter_fusion.1), calls=%async_computation.2 | async-start | bytes 2097152 | tf_op jit(solution)/shard_map/all_to_all | solution.py:133
  35.7 133.5 %all-to-all-start.1 = ((bf16[32,8,128,128]{3,2,1,0:T(8,128)(2,1)}), bf16[32,8,128,128]{3,2,1,0:T(8,128)(2,1)}, u32[]{:S(2)}, u32[]{:S(2)}) async-start(bf16[32,8,128,128]{3,2,1,0:T(8,128)(2,1)} %scatter_fusion), calls=%async_computation.1 | async-start | bytes 16777216 | tf_op jit(solution)/shard_map/all_to_all | solution.py:132
  177.9 6.2 %collective-permute-start = (bf16[8,8,512]{2,1,0:T(8,128)(2,1)S(1)}, bf16[8,8,512]{2,1,0:T(8,128)(2,1)S(1)}, u32[]{:S(2)}, u32[]{:S(2)}) collective-permute-start(bf16[8,8,512]{2,1,0:T(8,128)(2,1)S(1)} %get-tuple-element.34), channel_id=1, source_target_pairs={{0,16},{16,32},{32,48},{48,64},{64,80},{80,96},{96,112},{112,128},... | collective-permute-start | bytes 196616 | tf_op jit(solution)/shard_map/ppermute | solution.py:22
  179.9 6.2 %collective-permute-start.1 = (bf16[8,8,512]{2,1,0:T(8,128)(2,1)S(1)}, bf16[8,8,512]{2,1,0:T(8,128)(2,1)S(1)}, u32[]{:S(2)}, u32[]{:S(2)}) collective-permute-start(bf16[8,8,512]{2,1,0:T(8,128)(2,1)S(1)} %get-tuple-element.33), channel_id=1, source_target_pairs={{16,0},{32,16},{48,32},{64,48},{80,64},{96,80},{112,96},{128,112},... | collective-permute-start | bytes 196616 | tf_op jit(solution)/shard_map/ppermute | solution.py:25
  186.0 12.4 %copy-start.6 = (bf16[8,144,512]{2,1,0:T(8,128)(2,1)}, bf16[8,144,512]{2,1,0:T(8,128)(2,1)S(1)}, u32[]{:S(2)}) copy-start(bf16[8,144,512]{2,1,0:T(8,128)(2,1)S(1)} %constant_dynamic-update-slice_fusion) | copy-start | bytes 3538948
  224.5 8.3 %copy-start.7 = (s32[3,4]{1,0:T(4,128)S(1)}, s32[3,4]{1,0:T(4,128)}, u32[]{:S(2)}) copy-start(s32[3,4]{1,0:T(4,128)} %param.7) | copy-start | bytes 148
  225.7 35.6 %collective-permute-start.2 = (bf16[3,7,128,512]{2,3,1,0:T(8,128)(2,1)S(1)}, bf16[3,7,128,512]{2,3,1,0:T(8,128)(2,1)S(1)}, u32[]{:S(2)}, u32[]{:S(2)}) collective-permute-start(bf16[3,7,128,512]{2,3,1,0:T(8,128)(2,1)S(1)} %get-tuple-element.31), channel_id=1, source_target_pairs={{0,1},{1,2},{2,3},{3,4},{4,5},{5,6},{6,7},{7,8},{8,9},{9,10},{10,1... | collective-permute-start | bytes 8257544 | tf_op jit(solution)/shard_map/ppermute | solution.py:22
  227.7 35.4 %collective-permute-start.3 = (bf16[3,7,128,512]{2,3,1,0:T(8,128)(2,1)S(1)}, bf16[3,7,128,512]{2,3,1,0:T(8,128)(2,1)S(1)}, u32[]{:S(2)}, u32[]{:S(2)}) collective-permute-start(bf16[3,7,128,512]{2,3,1,0:T(8,128)(2,1)S(1)} %get-tuple-element.32), channel_id=1, source_target_pairs={{1,0},{2,1},{3,2},{4,3},{5,4},{6,5},{7,6},{8,7},{9,8},{10,9},{11,1... | collective-permute-start | bytes 8257544 | tf_op jit(solution)/shard_map/ppermute | solution.py:25
  264.3 8.0 %copy-start = (bf16[3,15,128,512]{2,3,1,0:T(8,128)(2,1)}, bf16[3,15,128,512]{2,3,1,0:T(8,128)(2,1)S(1)}, u32[]{:S(2)}) copy-start(bf16[3,15,128,512]{2,3,1,0:T(8,128)(2,1)S(1)} %get-tuple-element.29) | copy-start | bytes 17694724
  264.3 8.0 %copy-start.1 = (bf16[3,15,128,512]{2,3,1,0:T(8,128)(2,1)}, bf16[3,15,128,512]{2,3,1,0:T(8,128)(2,1)S(1)}, u32[]{:S(2)}) copy-start(bf16[3,15,128,512]{2,3,1,0:T(8,128)(2,1)S(1)} %get-tuple-element.30) | copy-start | bytes 17694724
  265.5 3.1 copy-start.3
  268.6 3.6 %copy-start.2 = (f32[8,128,512]{1,2,0:T(8,128)}, f32[8,128,512]{1,2,0:T(8,128)S(1)}, u32[]{:S(2)}) copy-start(f32[8,128,512]{1,2,0:T(8,128)S(1)} %get-tuple-element.24) | copy-start | bytes 6291460
  272.2 4.2 %copy-start.4 = (f32[8,128,512]{1,2,0:T(8,128)}, f32[8,128,512]{1,2,0:T(8,128)S(1)}, u32[]{:S(2)}) copy-start(f32[8,128,512]{1,2,0:T(8,128)S(1)} %get-tuple-element.12) | copy-start | bytes 6291460
where the time goes:
time: 328 us; the launch traced here: 327 us
  waiting for transfers between devices  159 us (48%)
  matrix products  48.4 us (15%)
  blocking collectives  38 us (12%)
  starting transfers between devices  31.2 us (10%)
  other arithmetic  26.9 us (8%)
  local copies, waits for them, and re-layouts  22.7 us (7%)
    all_to_all x1, waiting for transfers between devices, shards(): lax.all_to_all(outgoing, 'sky', split_axis=0, concat_axis=0, tiled=True)  122 us
    dot_general x3, matrix products, smooth(): jnp.einsum('vy,cyz->cvz', down_matrix, across, preferred_element_type=jnp...  38.1 us
    psum x1, blocking collectives, shards(): totals = lax.psum(powers, 'sky')  38 us
    ppermute x2, waiting for transfers between devices, extended(): lax.ppermute(lax.slice_in_dim(block, block.shape[dim] - width, None, axis...  28.7 us
    reduce_sum x4, other arithmetic, kernel_boxcars(): power = jnp.stack([jnp.sum(item * item, axis=(1, 2)) for item in found])  12 us
    max x1, other arithmetic, raise_score(): best = jnp.maximum(best, jnp.abs(running) * factor[width][:, None, None])  9.23 us
    ppermute x2, starting transfers between devices, extended(): lax.ppermute(lax.slice_in_dim(block, 0, width, axis=dim), axis, backward)  9.17 us
    dot_general x1, matrix products, block_values(): jnp.einsum('bs,scyx->bcyx', onehot, arrived, preferred_element_type=jnp.f...  8.3 us
  transfers between devices with their start and end apart: 7, of which 7 were waited for; matrix products, arithmetic and copies ran while one was open for 7% of the time, Pallas kernels for 0%

commit v1 on v0

--- a/solution.py
+++ b/solution.py
@@ -146,7 +146,7 @@
     best = jnp.zeros((channels, ROWB * block_size, COLB * block_size), jnp.float32)
     results = [kernel_boxcars(planes[kernel]) for kernel in range(KERNELS)]
     powers = jnp.stack([item[1] for item in results])
-    totals = lax.psum(powers, "sky")
+    totals = jnp.sum(lax.all_gather(powers, "sky"), axis=0)
     for kernel in range(KERNELS):
         best = raise_score(best, results[kernel][0], totals[kernel], clip_tenths[kernel], cells)
     return best

time: 328 us -> 316 us (0.963)
  blocking collectives: 38 us -> 23.5 us
    psum x1 -> x0, blocking collectives: 38 us -> none  [shards(): totals = lax.psum(powers, 'sky')]
    all_gather x0 -> x1, blocking collectives: none -> 23.5 us  [shards(): totals = jnp.sum(lax.all_gather(powers, 'sky'), axis=0)]
where the time goes in v1:
time: 316 us; the launch traced here: 312 us
  waiting for transfers between devices  159 us (50%)
  matrix products  48.4 us (15%)
  starting transfers between devices  31.2 us (10%)
  other arithmetic  27 us (9%)
  blocking collectives  23.5 us (7%)
  local copies, waits for them, and re-layouts  22.7 us (7%)
    all_to_all x1, waiting for transfers between devices, shards(): lax.all_to_all(outgoing, 'sky', split_axis=0, concat_axis=0, tiled=True)  122 us
    dot_general x3, matrix products, smooth(): jnp.einsum('vy,cyz->cvz', down_matrix, across, preferred_element_type=jnp...  38.1 us
    ppermute x2, waiting for transfers between devices, extended(): lax.ppermute(lax.slice_in_dim(block, block.shape[dim] - width, None, axis...  28.7 us
    all_gather x1, blocking collectives, shards(): totals = jnp.sum(lax.all_gather(powers, 'sky'), axis=0)  23.5 us
    reduce_sum x4, other arithmetic, kernel_boxcars(): power = jnp.stack([jnp.sum(item * item, axis=(1, 2)) for item in found])  12 us
    max x1, other arithmetic, raise_score(): best = jnp.maximum(best, jnp.abs(running) * factor[width][:, None, None])  9.23 us
    ppermute x2, starting transfers between devices, extended(): lax.ppermute(lax.slice_in_dim(block, 0, width, axis=dim), axis, backward)  9.17 us
    dot_general x1, matrix products, block_values(): jnp.einsum('bs,scyx->bcyx', onehot, arrived, preferred_element_type=jnp.f...  8.3 us
  transfers between devices with their start and end apart: 7, of which 7 were waited for; matrix products, arithmetic and copies ran while one was open for 7% of the time, Pallas kernels for 0%

profile of v1, /device:TPU:136, one launch (start us, length us, event | category | flops | bytes accessed | tf_op | source)
XLA Modules:
  0.0 312.2 jit_solution(9356636057249901801)
XLA Ops:
  0.0 0.0 copy-start.5
  0.0 0.7 and_select_fusion
  0.7 0.2 convert_reduce_fusion
  0.9 0.6 scatter_custom_fusion
  1.5 0.7 all_to_all.12
  2.2 7.4 %all-to-all-start = ((s32[16,2,1]{1,2,0:T(1,128)}), s32[16,2,1]{1,2,0:T(1,128)S(1)}, u32[]{:S(2)}, u32[]{:S(2)}) async-start(s32[16,2,1]{1,2,0:T(1,128)} %bitcast), calls=%async_computation | async-start | bytes 16384 | tf_op jit(solution)/shard_map/all_to_all | solution.py:134
  9.6 1.2 broadcast_in_dim.13
  10.8 2.4 scatter_fusion.1
  13.2 2.6 all-to-all-done
  15.8 4.9 %all-to-all-start.2 = ((bf16[32,128,128]{2,1,0:T(8,128)(2,1)}), bf16[32,128,128]{2,1,0:T(8,128)(2,1)S(1)}, u32[]{:S(2)}, u32[]{:S(2)}) async-start(bf16[32,128,128]{2,1,0:T(8,128)(2,1)} %scatter_fusion.1), calls=%async_computation.2 | async-start | bytes 2097152 | tf_op jit(solution)/shard_map/all_to_all | solution.py:133
  20.7 0.0 copy-done.5
  20.7 2.2 multiply_convert_fusion
  22.9 5.3 %broadcast_in_dim.12 = bf16[32,8,128,128]{3,2,1,0:T(8,128)(2,1)} broadcast(bf16[]{:T(256)} %constant.32.clone.1), dimensions={} | broadcast | bytes 8388610 | tf_op jit(solution)/shard_map/broadcast_in_dim | solution.py:121
  28.3 5.0 %scatter_fusion = bf16[32,8,128,128]{3,2,1,0:T(8,128)(2,1)} fusion(bf16[32,8,128,128]{3,2,1,0:T(8,128)(2,1)} %broadcast_in_dim.12, s32[8]{0:T(128)S(1)} %compare_select_fusion.2, bf16[8,8,128,128]{3,2,1,0:T(8,128)(2,1)S(1)} %multiply_convert_fusion), kind=kCustom, calls=%fused_computation.1 | custom fusion | bytes 6291488 | tf_op jit(solution)/shard_map/scatter | solution.py:123
  33.3 2.4 all-to-all-done.2
  35.7 5.9 %all-to-all-start.1 = ((bf16[32,8,128,128]{3,2,1,0:T(8,128)(2,1)}), bf16[32,8,128,128]{3,2,1,0:T(8,128)(2,1)}, u32[]{:S(2)}, u32[]{:S(2)}) async-start(bf16[32,8,128,128]{3,2,1,0:T(8,128)(2,1)} %scatter_fusion), calls=%async_computation.1 | async-start | bytes 16777216 | tf_op jit(solution)/shard_map/all_to_all | solution.py:132
  41.7 0.7 fusion.681
  42.4 0.7 fusion.680
  43.1 0.7 fusion.679
  43.8 0.5 broadcast.2173
  44.3 0.7 reduce.3
  45.0 0.1 eq.33
  45.1 0.2 convert_multiply_fusion.3
  45.4 2.0 fusion.25
  47.3 121.8 %all-to-all-done.1 = bf16[32,8,128,128]{3,2,1,0:T(8,128)(2,1)} async-done(((bf16[32,8,128,128]{3,2,1,0:T(8,128)(2,1)}), bf16[32,8,128,128]{3,2,1,0:T(8,128)(2,1)}, u32[]{:S(2)}, u32[]{:S(2)}) %all-to-all-start.1) | async-done | bytes 8388640 | tf_op jit(solution)/shard_map/all_to_all | solution.py:132
  169.2 8.3 %fusion.54 = bf16[8,1,128,4,128]{4,3,2,0,1:T(4,128)(2,1)S(1)} fusion(f32[4,128,128]{2,0,1:T(4,128)S(1)} %fusion.25, bf16[32,8,128,128]{3,2,1,0:T(8,128)(2,1)} %all-to-all-done.1, s32[32]{0:T(128)S(1)} %eq.33), kind=kOutput, calls=%fused_computation.165 | convolution fusion | flops 34603136 | bytes 9699456 | tf_op jit(solution)/shard_map/bs,scyx->bcyx/dot_general | solution.py:104
  177.5 0.4 reshape.273
  177.9 1.9 collective-permute-start
  179.9 4.1 %collective-permute-start.1 = (bf16[8,8,512]{2,1,0:T(8,128)(2,1)S(1)}, bf16[8,8,512]{2,1,0:T(8,128)(2,1)S(1)}, u32[]{:S(2)}, u32[]{:S(2)}) collective-permute-start(bf16[8,8,512]{2,1,0:T(8,128)(2,1)S(1)} %get-tuple-element.33), channel_id=1, source_target_pairs={{16,0},{32,16},{48,32},{64,48},{80,64},{96,80},{112,96},{128,112},... | collective-permute-start | bytes 196616 | tf_op jit(solution)/shard_map/ppermute | solution.py:25
  184.0 0.1 collective-permute-done
  184.1 0.1 constant_dynamic-update-slice_fusion.1
  184.2 1.8 collective-permute-done.1
  186.0 0.0 copy-start.6
  186.0 12.4 %convolution_convert_fusion.4 = bf16[8,512,128]{2,1,0:T(8,128)(2,1)S(1)} fusion(bf16[8,144,512]{2,1,0:T(8,128)(2,1)S(1)} %constant_dynamic-update-slice_fusion, bf16[]{:T(256)} %bitcast.61, bf16[]{:T(256)} %bitcast.62, bf16[]{:T(256)} %bitcast.63, bf16[]{:T(256)} %bitcast.64, bf16[]{:T(256)} %bitcast.65, bf16[]{:T(256)} %bitcast.67, bf16[]{:T(256)} %bitcast.66, ...), kind=kOutput, calls=%fused_computation.93 | convolution fusion | flops 767873024 | bytes 2228834 | tf_op jit(solution)/shard_map/vy,cyz->cvz/dot_general | solution.py:54
  198.4 0.0 copy-done.6
  198.4 12.2 %convolution_convert_fusion.5 = bf16[8,512,128]{2,1,0:T(8,128)(2,1)S(1)} fusion(bf16[8,144,512]{2,1,0:T(8,128)(2,1)S(1)} %constant_dynamic-update-slice_fusion, bf16[]{:T(256)} %bitcast.26, bf16[]{:T(256)} %bitcast.27, bf16[]{:T(256)} %bitcast.28, bf16[]{:T(256)} %bitcast.29, bf16[]{:T(256)} %bitcast.30, bf16[]{:T(256)} %bitcast.32, bf16[]{:T(256)} %bitcast.31, ...), kind=kOutput, calls=%fused_computation.94 | convolution fusion | flops 767873024 | bytes 2228834 | tf_op jit(solution)/shard_map/vy,cyz->cvz/dot_general | solution.py:54
  210.6 13.5 %convolution_convert_fusion.3 = bf16[8,512,128]{2,1,0:T(8,128)(2,1)S(1)} fusion(bf16[8,144,512]{2,1,0:T(8,128)(2,1)} %copy-done.6, bf16[]{:T(256)} %bitcast.84, bf16[]{:T(256)} %bitcast.85, bf16[]{:T(256)} %bitcast.86, bf16[]{:T(256)} %bitcast.87, bf16[]{:T(256)} %bitcast.88, bf16[]{:T(256)} %bitcast.90, bf16[]{:T(256)} %bitcast.89, bf16[]{:T(256)} %bitcast.74, ...), kind=kOutput, calls=%fused_computation.92 | convolution fusion | flops 767873024 | bytes 2228834 | tf_op jit(solution)/shard_map/vy,cyz->cvz/dot_general | solution.py:54
  224.1 0.3 pad_maximum_fusion.1
  224.5 0.0 copy-start.7
  224.5 1.2 fusion.677
  225.7 1.9 collective-permute-start.2
  227.7 5.1 %collective-permute-start.3 = (bf16[3,7,128,512]{2,3,1,0:T(8,128)(2,1)S(1)}, bf16[3,7,128,512]{2,3,1,0:T(8,128)(2,1)S(1)}, u32[]{:S(2)}, u32[]{:S(2)}) collective-permute-start(bf16[3,7,128,512]{2,3,1,0:T(8,128)(2,1)S(1)} %get-tuple-element.32), channel_id=1, source_target_pairs={{1,0},{2,1},{3,2},{4,3},{5,4},{6,5},{7,6},{8,7},{9,8},{10,9},{11,1... | collective-permute-start | bytes 8257544 | tf_op jit(solution)/shard_map/ppermute | solution.py:25
  232.8 0.0 copy-done.7
  232.8 28.6 %collective-permute-done.2 = bf16[3,7,128,512]{2,3,1,0:T(8,128)(2,1)S(1)} collective-permute-done((bf16[3,7,128,512]{2,3,1,0:T(8,128)(2,1)S(1)}, bf16[3,7,128,512]{2,3,1,0:T(8,128)(2,1)S(1)}, u32[]{:S(2)}, u32[]{:S(2)}) %collective-permute-start.2) | collective-permute-done | bytes 2752544 | tf_op jit(solution)/shard_map/ppermute | solution.py:22
  261.3 1.8 collective-permute-done.3
  263.1 1.2 maximum_maximum_fusion
  264.3 0.0 copy-start
  264.3 0.0 copy-start.1
  264.3 1.2 multiply_reduce_fusion.4
  265.5 0.0 copy-start.3
  265.5 3.1 multiply_reduce_fusion.8
  268.6 0.0 copy-start.2
  268.6 0.0 copy-done.3
  268.6 3.6 %multiply_reduce_fusion.7 = (f32[8]{0:T(128)S(1)}, f32[8,128,512]{1,2,0:T(8,128)S(1)}, f32[8]{0:T(128)S(1)}, f32[8,128,512]{1,2,0:T(8,128)}) fusion(bf16[3,15,128,512]{2,3,1,0:T(8,128)(2,1)S(1)} %get-tuple-element.30, bf16[3,15,128,512]{2,3,1,0:T(8,128)(2,1)S(1)} %get-tuple-element.29, bf16[8,512,128]{2,1,0:T(8,128)(2,1)S(1)} %convolution_convert_fusion.5, ...), kind=kLoop, calls=%fused_computation.85 | loop fusion | flops 17301488 | bytes 22020160 | tf_op jit(solution)/shard_map/reduce_sum | solution.py:76
  272.2 0.0 copy-start.4
  272.2 0.0 copy-done
  272.2 0.0 copy-done.1
  272.2 0.0 copy-done.2
  272.2 4.1 %multiply_reduce_fusion.6 = (f32[8]{0:T(128)S(1)}, f32[8,128,512]{1,2,0:T(8,128)}, f32[8]{0:T(128)S(1)}, f32[8,128,512]{1,2,0:T(8,128)}) fusion(bf16[3,15,128,512]{2,3,1,0:T(8,128)(2,1)S(1)} %get-tuple-element.30, bf16[3,15,128,512]{2,3,1,0:T(8,128)(2,1)S(1)} %get-tuple-element.29, f32[8,128,512]{1,2,0:T(8,128)S(1)} %get-tuple-element.12, ...), kind=kLoop, calls=%fused_computation.84 | loop fusion | flops 18874352 | bytes 25165888 | tf_op jit(solution)/shard_map/reduce_sum | solution.py:76
  276.4 0.0 copy-done.4
  276.4 23.5 %all-gather = f32[48,4,8]{2,1,0:T(4,128)S(1)} all-gather(f32[3,4,8]{2,1,0:T(4,128)S(1)} %pad_maximum_fusion.2), channel_id=2, replica_groups=mesh['sky'=16,'freq'=16] {'sky'}, dimensions={0}, use_global_device_ids=true | all-gather | bytes 6528 | tf_op jit(solution)/shard_map/all_gather | solution.py:149
  300.0 0.1 fusion.554
  300.1 9.2 %fusion.14 = f32[8,128,512]{1,2,0:T(8,128)} fusion(f32[8,128,512]{1,2,0:T(8,128)} %get-tuple-element.26, f32[8,128,512]{1,2,0:T(8,128)} %copy-done.2, f32[8,128,512]{1,2,0:T(8,128)} %get-tuple-element.28, f32[8,128,512]{1,2,0:T(8,128)} %copy-done.3, f32[8,128,512]{1,2,0:T(8,128)} %get-tuple-element.14, f32[8,128,512]{1,2,0:T(8,128)} %copy-done.4, ...), kind=kLoop, calls=%fused_computation.31 | loop fusion | flops 26738688 | bytes 24117632 | tf_op jit(solution)/shard_map/max | solution.py:84
  309.3 2.9 copy.18
  (17 shorter events, 0.2 us)
Async XLA Ops:
  0.0 20.7 %copy-start.5 = (bf16[8,128,128]{2,1,0:T(8,128)(2,1)S(1)}, bf16[8,128,128]{2,1,0:T(8,128)(2,1)}, u32[]{:S(2)}) copy-start(bf16[8,128,128]{2,1,0:T(8,128)(2,1)} %param.5) | copy-start | bytes 786436
  2.2 13.6 %all-to-all-start = ((s32[16,2,1]{1,2,0:T(1,128)}), s32[16,2,1]{1,2,0:T(1,128)S(1)}, u32[]{:S(2)}, u32[]{:S(2)}) async-start(s32[16,2,1]{1,2,0:T(1,128)} %bitcast), calls=%async_computation | async-start | bytes 16384 | tf_op jit(solution)/shard_map/all_to_all | solution.py:134
  15.8 19.9 %all-to-all-start.2 = ((bf16[32,128,128]{2,1,0:T(8,128)(2,1)}), bf16[32,128,128]{2,1,0:T(8,128)(2,1)S(1)}, u32[]{:S(2)}, u32[]{:S(2)}) async-start(bf16[32,128,128]{2,1,0:T(8,128)(2,1)} %scatter_fusion.1), calls=%async_computation.2 | async-start | bytes 2097152 | tf_op jit(solution)/shard_map/all_to_all | solution.py:133
  35.7 133.5 %all-to-all-start.1 = ((bf16[32,8,128,128]{3,2,1,0:T(8,128)(2,1)}), bf16[32,8,128,128]{3,2,1,0:T(8,128)(2,1)}, u32[]{:S(2)}, u32[]{:S(2)}) async-start(bf16[32,8,128,128]{3,2,1,0:T(8,128)(2,1)} %scatter_fusion), calls=%async_computation.1 | async-start | bytes 16777216 | tf_op jit(solution)/shard_map/all_to_all | solution.py:132
  177.9 6.2 %collective-permute-start = (bf16[8,8,512]{2,1,0:T(8,128)(2,1)S(1)}, bf16[8,8,512]{2,1,0:T(8,128)(2,1)S(1)}, u32[]{:S(2)}, u32[]{:S(2)}) collective-permute-start(bf16[8,8,512]{2,1,0:T(8,128)(2,1)S(1)} %get-tuple-element.34), channel_id=1, source_target_pairs={{0,16},{16,32},{32,48},{48,64},{64,80},{80,96},{96,112},{112,128},... | collective-permute-start | bytes 196616 | tf_op jit(solution)/shard_map/ppermute | solution.py:22
  179.9 6.2 %collective-permute-start.1 = (bf16[8,8,512]{2,1,0:T(8,128)(2,1)S(1)}, bf16[8,8,512]{2,1,0:T(8,128)(2,1)S(1)}, u32[]{:S(2)}, u32[]{:S(2)}) collective-permute-start(bf16[8,8,512]{2,1,0:T(8,128)(2,1)S(1)} %get-tuple-element.33), channel_id=1, source_target_pairs={{16,0},{32,16},{48,32},{64,48},{80,64},{96,80},{112,96},{128,112},... | collective-permute-start | bytes 196616 | tf_op jit(solution)/shard_map/ppermute | solution.py:25
  186.0 12.4 %copy-start.6 = (bf16[8,144,512]{2,1,0:T(8,128)(2,1)}, bf16[8,144,512]{2,1,0:T(8,128)(2,1)S(1)}, u32[]{:S(2)}) copy-start(bf16[8,144,512]{2,1,0:T(8,128)(2,1)S(1)} %constant_dynamic-update-slice_fusion) | copy-start | bytes 3538948
  224.5 8.3 %copy-start.7 = (s32[3,4]{1,0:T(4,128)S(1)}, s32[3,4]{1,0:T(4,128)}, u32[]{:S(2)}) copy-start(s32[3,4]{1,0:T(4,128)} %param.7) | copy-start | bytes 148
  225.7 35.6 %collective-permute-start.2 = (bf16[3,7,128,512]{2,3,1,0:T(8,128)(2,1)S(1)}, bf16[3,7,128,512]{2,3,1,0:T(8,128)(2,1)S(1)}, u32[]{:S(2)}, u32[]{:S(2)}) collective-permute-start(bf16[3,7,128,512]{2,3,1,0:T(8,128)(2,1)S(1)} %get-tuple-element.31), channel_id=1, source_target_pairs={{0,1},{1,2},{2,3},{3,4},{4,5},{5,6},{6,7},{7,8},{8,9},{9,10},{10,1... | collective-permute-start | bytes 8257544 | tf_op jit(solution)/shard_map/ppermute | solution.py:22
  227.7 35.4 %collective-permute-start.3 = (bf16[3,7,128,512]{2,3,1,0:T(8,128)(2,1)S(1)}, bf16[3,7,128,512]{2,3,1,0:T(8,128)(2,1)S(1)}, u32[]{:S(2)}, u32[]{:S(2)}) collective-permute-start(bf16[3,7,128,512]{2,3,1,0:T(8,128)(2,1)S(1)} %get-tuple-element.32), channel_id=1, source_target_pairs={{1,0},{2,1},{3,2},{4,3},{5,4},{6,5},{7,6},{8,7},{9,8},{10,9},{11,1... | collective-permute-start | bytes 8257544 | tf_op jit(solution)/shard_map/ppermute | solution.py:25
  264.3 8.0 %copy-start = (bf16[3,15,128,512]{2,3,1,0:T(8,128)(2,1)}, bf16[3,15,128,512]{2,3,1,0:T(8,128)(2,1)S(1)}, u32[]{:S(2)}) copy-start(bf16[3,15,128,512]{2,3,1,0:T(8,128)(2,1)S(1)} %get-tuple-element.29) | copy-start | bytes 17694724
  264.3 8.0 %copy-start.1 = (bf16[3,15,128,512]{2,3,1,0:T(8,128)(2,1)}, bf16[3,15,128,512]{2,3,1,0:T(8,128)(2,1)S(1)}, u32[]{:S(2)}) copy-start(bf16[3,15,128,512]{2,3,1,0:T(8,128)(2,1)S(1)} %get-tuple-element.30) | copy-start | bytes 17694724
  265.5 3.1 copy-start.3
  268.6 3.6 %copy-start.2 = (f32[8,128,512]{1,2,0:T(8,128)}, f32[8,128,512]{1,2,0:T(8,128)S(1)}, u32[]{:S(2)}) copy-start(f32[8,128,512]{1,2,0:T(8,128)S(1)} %get-tuple-element.24) | copy-start | bytes 6291460
  272.2 4.2 %copy-start.4 = (f32[8,128,512]{1,2,0:T(8,128)}, f32[8,128,512]{1,2,0:T(8,128)S(1)}, u32[]{:S(2)}) copy-start(f32[8,128,512]{1,2,0:T(8,128)S(1)} %get-tuple-element.12) | copy-start | bytes 6291460
